TPU v7x, 32 devices: a whole 2x2x4 slice. The times are simulated.
32 devices in a mesh: dom: 8 (over y, x, core), tool: 4 (over z).
Axes of the slice: x: 2, y: 2, z: 4, core: 2. Of those that a mesh axis runs over, the one named last changes fastest.
Arguments:
- records: float32 [2048, 512], P(('dom', 'tool')), may hold values from -6 to 6
- tool_data: float32 [8192, 512], P(('dom', 'tool')), may hold values from -6 to 6
- owners: int32 [2048, 2], P(('dom', 'tool')), may hold values from 0 to 31, all different within a row; in each aligned block of 64 rows (0 to 63, 64 to 127, ...) at most 6 rows name the same one
- local_seg: int32 [2048, 2], P(('dom', 'tool')), may hold values from 0 to 255
- active: int32 [2048, 64], P(('dom', 'tool')), may hold values 0 or 1
- stiffness: float32 [2048, 5, 4096], P(('dom', 'tool')), may hold values from -0.3125 to 0.3125
- columns: int32 [2048, 5], P(('dom', 'tool')), may hold values from 0 to 67, as said below
- vectors: float32 [2048, 4096], P(('dom', 'tool')), may hold values from -6 to 6
Outputs:
- product: float32 [2048, 4096], P(('dom', 'tool'))
Inputs may be any that keep to these rules, and one draw needn't show every extreme that they name: Among the 64 node blocks of one device no owner is named by more than 6 candidates, a bound that some block reaches; a block's candidates name different owners. `columns`: the first column of each row is the row's own block, column 2 + b mod 64; the others lie within 2 blocks of it.
All inputs are finite; a program needn't handle non-finite values. No bound on the sum of `active` on one device may be relied on, other than what follows from the above.
Results may differ from a plain program's by a relative error of at most 0.0003.
Values sent between devices are 32-bit elements; how exact they have to be, the bound alone decides.
No kernel may reach another device: no remote copies, remote signals or barrier semaphores. Data moves between devices by JAX's collectives and lax.ppermute only.
A program may use at most 128 MiB of HBM per device.

v0:
```python
import functools
import math

import jax
import jax.numpy as jnp
from jax import lax
from jax.experimental import pallas as pl
from jax.experimental.pallas import tpu as pltpu
from jax.sharding import PartitionSpec as P

NODE = 64
NVEC = 64
FIELDS = 8
HB = 2
LANES = 128
SUB = 8
AXES = ("dom", "tool")
TURN = 1.0 / (2.0 * math.pi)
REACH = math.sqrt(math.log2(math.e) / 4.0)
SHARE = math.sqrt(0.05)
FAR = -1e30
SINE = (6.283164044071425, -41.33714233428813, 81.34076747811504, -70.99341826772617)
LIFT = math.log2(-SINE[3] * SHARE * 0.5)
F32 = jnp.float32
BF16 = jnp.bfloat16
VMEM = pl.BlockSpec(memory_space=pltpu.VMEM)
SMEM = pl.BlockSpec(memory_space=pltpu.SMEM)
HBM = pl.BlockSpec(memory_space=pltpu.HBM)
ROUND = 1.5 * 2.0**23
PARTS = 3


def params(mib):
    return pltpu.CompilerParams(vmem_limit_bytes=mib << 20)


def left_half(rows):
    return lax.broadcasted_iota(jnp.int32, (rows, LANES), 1) < NODE


def swap(x):
    return pltpu.roll(x, NODE, 1)


def split(x):
    high = x.astype(BF16)
    return high, (x - high.astype(F32)).astype(BF16)


def three(x):
    high = x.astype(BF16).astype(F32)
    rest = x - high
    mid = rest.astype(BF16).astype(F32)
    return high, mid, rest - mid


def fold(out, half):
    pairs = NODE // 2
    even, odd = out[:pairs], out[pairs:]
    return jnp.where(half, even, odd) + swap(jnp.where(half, odd, even))


def flip(tiles):
    tiles = list(tiles)
    row = lax.broadcasted_iota(jnp.int32, (SUB, LANES), 0)
    for d in (4, 2, 1):
        keep = (row & d) == 0
        for i in range(SUB):
            if i & d:
                continue
            a, b = tiles[i], tiles[i + d]
            if 2 * d == SUB:
                moved = pltpu.roll(jnp.where(keep, b, a), d, 0)
                tiles[i], tiles[i + d] = jnp.where(keep, a, moved), jnp.where(keep, moved, b)
            else:
                tiles[i] = jnp.where(keep, a, pltpu.roll(b, d, 0))
                tiles[i + d] = jnp.where(keep, pltpu.roll(a, SUB - d, 0), b)
    return tiles


def flip_all(tiles):
    runs = [flip(tiles[i : i + SUB]) for i in range(0, len(tiles), SUB)]
    return [jnp.concatenate([run[j] for run in runs], axis=0) for j in range(SUB)]


def tiles_from(blocks):
    out = []
    for at in range(0, blocks[0].shape[0], SUB):
        out += flip([x[at : at + SUB] for x in blocks])
    return out


def doubled(x, half):
    other = swap(x)
    return jnp.where(half, x, other), jnp.where(half, other, x)


def high_low(x, half):
    return jnp.where(half, x, x - x.astype(BF16).astype(F32))


def copies_of(sources, targets, sems):
    made = [pltpu.make_async_copy(a, b, sems.at[i]) for i, (a, b) in enumerate(zip(sources, targets))]
    for copy in made:
        copy.start()
    return made


def pair_fields(x, y):
    quarter = left_half(x.shape[0])
    return jnp.concatenate([jnp.where(quarter, x, swap(y)), jnp.where(quarter, swap(x), y)], axis=0)


def field_rows(shape):
    row = lax.broadcasted_iota(jnp.int32, shape, 0)
    place = (row < 2) | (row == 4)
    return row, place, (row != 7) & ~place


def ranks(hits):
    n = hits.shape[1]
    upper = (
        lax.broadcasted_iota(jnp.int32, (n, n), 0) <= lax.broadcasted_iota(jnp.int32, (n, n), 1)
    ).astype(BF16)
    return jnp.dot(hits.astype(F32).astype(BF16), upper, preferred_element_type=F32)


def prep_kernel(
    doms, peers, capacity, stride, owners_hbm, seg_hbm, vec_hbm, send_ref, slot_hbm,
    owners_ref, seg_ref, first_ref, last_ref, edge_ref, slot_ref, sems,
):
    last = vec_hbm.shape[0] - 1
    got = copies_of(
        (owners_hbm, seg_hbm, vec_hbm.at[0], vec_hbm.at[last]), (owners_ref, seg_ref, first_ref, last_ref), sems
    )
    got[0].wait()
    got[1].wait()
    cands, blocks = owners_ref.shape
    pairs = NODE // 2
    share = 2 * HB * pairs // peers
    place = lax.broadcasted_iota(jnp.int32, (peers, blocks), 0)
    owner_ids = place % doms * (peers // doms) + place // doms
    lanes = lax.broadcasted_iota(jnp.int32, (peers, LANES), 1)
    send = jnp.zeros((peers, LANES), F32)
    before = jnp.zeros((peers, 1), F32)
    for k in range(cands):
        target = owners_ref[k : k + 1, :]
        hits = owner_ids == jnp.broadcast_to(target, (peers, blocks))
        places = jnp.where(hits, before + ranks(hits) - 1.0, -1.0)
        before = before + jnp.sum(hits.astype(F32), axis=1, keepdims=True)
        rank = jnp.sum(jnp.maximum(places, 0.0), axis=0, keepdims=True)
        slot_ref[k : k + 1, :] = target * stride + rank.astype(jnp.int32)
        wanted = jnp.broadcast_to(seg_ref[k : k + 1, :].astype(F32), (peers, blocks))
        for s in range(capacity):
            named = jnp.sum(jnp.where(places == float(s), wanted, 0.0), axis=1, keepdims=True)
            send = send + jnp.where(lanes == s, named, 0.0)
    slots = pltpu.make_async_copy(slot_ref, slot_hbm, sems.at[4])
    slots.start()
    send_ref[pl.ds(0, peers, stride=1 + share), :] = send
    got[2].wait()
    got[3].wait()
    for h in range(HB):
        edge_ref[h * pairs : (h + 1) * pairs, :] = first_ref[pl.ds(h, pairs, stride=SUB), :]
        edge_ref[(HB + h) * pairs : (HB + h + 1) * pairs, :] = last_ref[pl.ds(SUB - HB + h, pairs, stride=SUB), :]
    for r in range(share):
        send_ref[pl.ds(1 + r, peers, stride=1 + share), :] = edge_ref[pl.ds(r, peers, stride=share), :]
    slots.wait()


def turn_kernel(doms, tools, in_ref, out_ref):
    rows = in_ref.shape[0] // (doms * tools)
    for t in range(tools):
        for d in range(doms):
            source, target = (t * doms + d) * rows, (d * tools + t) * rows
            out_ref[target : target + rows, :] = in_ref[source : source + rows, :]


def rows_kernel(peers, capacity, stride, got_ref, part_ref, out_ref):
    segs, width = part_ref.shape[0], part_ref.shape[1] // PARTS
    chunks = width // LANES
    share = got_ref.shape[0] // peers - 1
    seg = lax.broadcasted_iota(jnp.int32, (peers, segs), 1)
    want = got_ref[pl.ds(0, peers, stride=1 + share), :].astype(jnp.int32)
    picks = jnp.concatenate([(seg == want[:, s : s + 1]).astype(F32).astype(BF16) for s in range(capacity)], axis=0)
    for c in range(chunks):
        got = None
        for p in range(PARTS):
            at = p * width + c * LANES
            term = jnp.dot(picks, part_ref[:, at : at + LANES], preferred_element_type=F32)
            got = term if got is None else got + term
        for s in range(capacity):
            out_ref[pl.ds(s * chunks + c, peers, stride=stride * chunks), :] = got[s * peers : (s + 1) * peers]
    me = lax.axis_index(AXES[1]) * lax.axis_size(AXES[0]) + lax.axis_index(AXES[0])
    peer = lax.broadcasted_iota(jnp.int32, (peers, LANES), 0)
    for r in range(share):
        edge = got_ref[pl.ds(1 + r, peers, stride=1 + share), :]
        following = jnp.where(peer == peers - 1, 0.0, pltpu.roll(edge, peers - 1, 0))
        previous = jnp.where(peer == 0, 0.0, pltpu.roll(edge, 1, 0))
        out_ref[pl.ds(capacity * chunks + r, peers, stride=stride * chunks), :] = jnp.where(
            me < peers // 2, following, previous
        )


def parts_kernel(after_prep, tool_hbm, part_ref, tool_ref, sems):
    copies_of((tool_hbm,), (tool_ref,), sems)[0].wait()
    width = tool_ref.shape[1]
    for p, part in enumerate(three(tool_ref[...])):
        part_ref[:, p * width : (p + 1) * width] = part.astype(BF16)


def ordered(row, h, m, l, order):
    out = jnp.zeros(row.shape, F32)
    for value, name in ((h, "h"), (m, "m"), (l, "l")):
        for i, at in enumerate(order):
            if at == name:
                out = jnp.where(row == i, value, out)
    return out


def main_kernel(
    columns_hbm, vec_hbm, rec_hbm, act_hbm, stiff_hbm, out_hbm, own_hbm, field_ref, slip_ref, edge_ref, rest_ref,
    columns_ref, vec_ref, rec_ref, act_ref, stiff_ref, wide_ref, left_ref, last_ref, out_ref, own_ref, sems, out_sems,
):
    nnz, groups = stiff_ref.shape[:2]
    blocks = groups * SUB
    pairs = NODE // 2
    even_count = nnz // 2 * 2
    half = left_half(SUB)
    half_rows = left_half(pairs)
    got = copies_of(
        (columns_hbm, vec_hbm, rec_hbm, act_hbm) + tuple(stiff_hbm.at[:, g] for g in range(groups)),
        (columns_ref, vec_ref, rec_ref, act_ref) + tuple(stiff_ref.at[:, g] for g in range(groups)),
        sems,
    )
    zero = jnp.zeros((NODE, LANES), BF16)
    for h in range(HB):
        wide_ref[h] = zero
        wide_ref[blocks + HB + h] = zero

    def tile(m):
        return pl.ds(m * SUB, SUB)

    def spread(g):
        for at in range(0, pairs, 2 * SUB):
            evens, odds = [], []
            for m in range(at, at + 2 * SUB):
                even, odd = doubled(vec_ref[g, tile(m), :], half)
                evens.append(high_low(even, half))
                odds.append(high_low(odd, half))
            for q, values in enumerate((evens, odds)):
                for j, x in enumerate(flip_all(values)):
                    own_ref[g * SUB + j, q * pairs + at : q * pairs + at + 2 * SUB, :] = x.astype(BF16)
            mixed = [x for both in zip(evens, odds) for x in both]
            for j, x in enumerate(flip_all(mixed)):
                wide_ref[HB + g * SUB + j, 2 * at : 2 * at + 4 * SUB, :] = x.astype(BF16)

    row, place, _ = field_rows((SUB, LANES))
    scale = jnp.where(place, REACH, 1.0)
    lane = lax.broadcasted_iota(jnp.int32, (SUB, LANES), 1)
    turn = lane // NODE * NODE + lane % pairs * 2 + lane % NODE // pairs

    def evens_first(x):
        return jnp.take_along_axis(x, turn, axis=1, mode="promise_in_bounds")

    def fields(g):
        for j in range(0, SUB, 2):
            x = rec_ref[g, pl.ds(j, FIELDS // 2, stride=SUB), :]
            y = rec_ref[g, pl.ds(j + 1, FIELDS // 2, stride=SUB), :]
            part = pair_fields(x, y) * scale
            norm = -0.5 * jnp.sum(jnp.where(place, part * part, 0.0), axis=0, keepdims=True)
            at = g * SUB + j
            flags = jnp.concatenate([act_ref[pl.ds(at, 1), :], act_ref[pl.ds(at + 1, 1), :]], axis=1)
            norm = jnp.where(flags == 0, FAR, norm)
            h, m, l = three(evens_first(part))
            extra = ordered(row, *three(evens_first(jnp.broadcast_to(norm, (SUB, LANES)))), "hml")
            extra = jnp.where((row > 2) & (row < 6), 1.0, extra)
            slip = ordered(row, h[7:8], m[7:8], l[7:8], "hhmhlm")
            none = jnp.zeros((SUB, LANES), F32)
            more = jnp.zeros((LANES - 10 * SUB, LANES), F32)
            stack = jnp.concatenate([h, h, m, h, l, m, extra, none, slip, swap(slip), more], axis=0).T
            field_ref[at] = stack[:NODE].astype(BF16)
            field_ref[at + 1] = stack[NODE:].astype(BF16)
            slip_ref[at // 2] = swap(stack[:NODE]).astype(BF16)

    def prepare(g):
        for at in range(0, pairs, 2 * SUB):
            for e in range(0, nnz, 2):
                evens, odds = [], []
                for m in range(at, at + 2 * SUB):
                    x = stiff_ref[e, g, tile(m), :]
                    if e < even_count:
                        y = stiff_ref[e + 1, g, tile(m), :]
                        evens.append(jnp.where(half, x, swap(y)))
                        odds.append(jnp.where(half, swap(x), y))
                    else:
                        even, odd = doubled(x, half)
                        evens.append(high_low(even, half))
                        odds.append(high_low(odd, half))
                for q, values in enumerate((evens, odds)):
                    rows = slice(q * pairs + at, q * pairs + at + 2 * SUB)
                    for j, x in enumerate(flip_all(values)):
                        if e < even_count:
                            high, low = split(x)
                            cols = slice(e * NODE, (e + 2) * NODE)
                            left_ref[j, rows, cols] = high
                            left_ref[j, NODE + rows.start : NODE + rows.stop, cols] = low
                        else:
                            last_ref[j, rows, :] = x.astype(BF16)

    def product(g):
        folded = []
        for j in range(SUB):
            cols = [wide_ref[columns_ref[e, g * SUB + j]] for e in range(nnz)]
            folded.append(fold(times(left_ref[j], last_ref[j], cols), half_rows))
        for m, x in enumerate(tiles_from(folded)):
            out_ref[g, m * SUB : (m + 1) * SUB, :] = x

    got[1].wait()
    spread(0)
    spread(1)
    got[4].wait()
    prepare(0)
    for h in range(HB):
        edge_ref[h] = left_ref[h]
        rest_ref[h] = last_ref[h]
    got[0].wait()
    got[2].wait()
    got[3].wait()

    def body(g, carry):
        pltpu.make_async_copy(stiff_hbm.at[:, g + 1], stiff_ref.at[:, g + 1], sems.at[5 + g]).wait()
        product(g)
        prepare(g + 1)
        spread(jnp.minimum(g + 2, groups - 1))
        fields(g)
        return carry

    lax.fori_loop(0, groups - 1, body, 0)
    owns = pltpu.make_async_copy(own_ref, own_hbm, out_sems.at[0])
    owns.start()
    product(groups - 1)
    inners = pltpu.make_async_copy(out_ref, out_hbm, out_sems.at[1])
    inners.start()
    fields(groups - 1)
    for h in range(HB):
        edge_ref[HB + h] = left_ref[SUB - HB + h]
        rest_ref[HB + h] = last_ref[SUB - HB + h]
    owns.wait()
    inners.wait()


def times(left, last, cols):
    even_count = left.shape[1] // NODE
    out = jnp.dot(left, jnp.concatenate(cols[:even_count], axis=0), preferred_element_type=F32)
    out = out[:NODE] + out[NODE:]
    if len(cols) > even_count:
        out = out + jnp.dot(last, jnp.concatenate([cols[-1], cols[-1]], axis=0), preferred_element_type=F32)
    return out


def contact_kernel(
    doms, tools, capacity, stride,
    slot_hbm, columns_hbm, own_hbm, inner_hbm, rows_ref, field_ref, slip_ref, edge_ref, rest_ref, out_ref,
    slot_ref, columns_ref, own_ref, inner_ref, tall_ref, gram_ref, halo_ref, wide_ref, hold_ref, delta_ref, sems, own_sems, inner_sems,
):
    got = copies_of((columns_hbm, slot_hbm), (columns_ref, slot_ref), sems)
    nnz, blocks = columns_ref.shape
    groups = blocks // SUB
    peers = doms * tools

    def own_copy(g):
        spot = pl.ds(g * SUB, SUB)
        return pltpu.make_async_copy(own_hbm.at[spot], own_ref.at[spot], own_sems.at[g])

    def inner_copy(g):
        return pltpu.make_async_copy(inner_hbm.at[g], inner_ref.at[g], inner_sems.at[g])

    for g in range(groups):
        own_copy(g).start()
        inner_copy(g).start()
    pairs = NODE // 2
    half = left_half(pairs)
    full = left_half(NODE)
    row, place, angle = field_rows((SUB, LANES))
    scale = jnp.where(place, REACH, jnp.where(row == 3, TURN, jnp.where(angle, 3.0 * TURN, 1.0)))
    none = jnp.zeros((SUB, LANES), F32)

    def tile_of(reach, phase, slip):
        turn = jnp.abs(phase - ((phase + ROUND) - ROUND)) - 0.25
        square = turn * turn
        wave = square + SINE[2] / SINE[3]
        wave = wave * square + SINE[1] / SINE[3]
        wave = wave * square + SINE[0] / SINE[3]
        return jnp.exp2(reach) * (wave * turn) * (2.0 + jnp.tanh(slip))

    def tiles(g):
        raws, slips = [], []
        for j in range(SUB):
            b = g * SUB + j
            tool = pair_fields(rows_ref[slot_ref[0, b]], rows_ref[slot_ref[1, b]]) * scale
            norm = LIFT - 0.5 * jnp.sum(jnp.where(place, tool * tool, 0.0), axis=0, keepdims=True)
            h, m, l = three(tool)
            extra = jnp.where(row < 3, 1.0, 0.0) + ordered(row, *three(norm), "---hml")
            right = []
            for mask, more in ((place, extra), (angle, none)):
                hm, mm, lm = (jnp.where(mask, v, 0.0) for v in (h, m, l))
                right.append(jnp.concatenate([hm, mm, hm, lm, hm, mm, more, none], axis=0).astype(BF16))
            right = jnp.concatenate(right, axis=1)
            raws.append(jnp.dot(field_ref[b][:, : right.shape[0]], right, preferred_element_type=F32))
            slips.append(ordered(row, h[7:8], m[7:8], l[7:8], "hmhlhm"))
            if j % 2:
                right = jnp.concatenate(
                    [jnp.concatenate([slips[j - 1], none], axis=1), jnp.concatenate([none, slips[j]], axis=1)], axis=0
                ).astype(BF16)
                slide = jnp.dot(slip_ref[b // 2][:, : 2 * SUB], right, preferred_element_type=F32)
                for i in range(2):
                    raw = raws[j - 1 + i]
                    high, low = split(tile_of(raw[:, :LANES], raw[:, LANES:], slide[:, i * LANES : (i + 1) * LANES]))
                    tall_ref[j - 1 + i, :NODE, :] = high
                    tall_ref[j - 1 + i, NODE:, :] = low

    def grams(g):
        for j in range(SUB):
            tall = tall_ref[j]
            gram = lax.dot_general(tall, tall, (((1,), (1,)), ((), ())), preferred_element_type=F32)
            gram = gram[:NODE] + gram[NODE:]
            gram_ref[j] = high_low(gram + swap(gram), full).astype(BF16)

    def apply(g):
        own_copy(g).wait()
        inner_copy(g).wait()
        folded = []
        for j in range(SUB):
            own = own_ref[g * SUB + j]
            out = jnp.dot(gram_ref[j], jnp.concatenate([own, own], axis=0), preferred_element_type=F32)
            folded.append(fold(out, half))
        for m, x in enumerate(tiles_from(folded)):
            spot = slice(m * SUB, (m + 1) * SUB)
            out_ref[g, spot, :] = inner_ref[g, spot, :] + x

    def halo():
        share = 2 * HB * pairs // peers
        step = min(share, rows_ref.shape[1])
        for at in range(0, 2 * HB * pairs, step):
            q, r = at // share, at % share
            p = q % doms * tools + q // doms
            halo_ref[at : at + step, :] = rows_ref[p * stride + capacity + r // step][:step]
        for h in range(2 * HB):
            even, odd = doubled(halo_ref[h * pairs : (h + 1) * pairs, :], half)
            hold_ref[h, pl.ds(0, pairs, stride=2), :] = even
            hold_ref[h, pl.ds(1, pairs, stride=2), :] = odd
            wide_ref[h] = high_low(hold_ref[h], full).astype(BF16)
        wide_ref[2 * HB] = jnp.zeros((NODE, LANES), BF16)
        got[0].wait()
        deltas = []
        for i in range(2 * HB):
            b = i if i < HB else blocks - 2 * HB + i
            cols = []
            for e in range(nnz):
                c = columns_ref[e, b]
                ahead, behind = c - blocks - HB, c + HB
                cols.append(wide_ref[jnp.where(c < HB, behind, jnp.where(ahead >= 0, ahead, 2 * HB))])
            deltas.append(fold(times(edge_ref[i], rest_ref[i], cols), half))
        return deltas

    deltas = halo()
    for i, delta in enumerate(deltas):
        delta_ref[i] = delta
    got[1].wait()
    tiles(0)
    grams(0)
    tiles(1)

    def body(g, carry):
        apply(g - 2)
        grams(g - 1)
        tiles(g)
        return carry

    lax.fori_loop(2, groups, body, 0)
    apply(groups - 2)
    grams(groups - 1)
    apply(groups - 1)
    for i in range(2 * HB):
        g, j = (0, i) if i < HB else (groups - 1, SUB - 2 * HB + i)
        spot = pl.ds(j, pairs, stride=SUB)
        out_ref[g, spot, :] = out_ref[g, spot, :] + delta_ref[i]


def per_device(records, tool_data, owners, local_seg, active, stiffness, columns, vectors):
    doms, tools = (lax.axis_size(axis) for axis in AXES)
    peers = doms * tools
    blocks, cands = owners.shape
    nnz = columns.shape[1]
    segs, width = tool_data.shape
    capacity = max(2, (3 * blocks * cands + 2 * peers - 1) // (2 * peers))
    groups = blocks // SUB
    pairs = NODE // 2
    chunks = width // LANES
    i32 = jnp.int32

    def shape(dims, dtype=F32):
        return jax.ShapeDtypeStruct(dims, dtype)

    def tiles_of(x, rows):
        lead = x.shape[:-2]
        n = len(lead)
        x = x.reshape(lead + (rows // SUB, SUB, x.shape[-1] // LANES, LANES))
        x = jnp.swapaxes(x, n + 1, n + 2)
        return x.reshape(lead + (rows // SUB, -1, LANES))

    vec = tiles_of(vectors, blocks)
    rec = tiles_of(records, blocks)
    stiff = tiles_of(jnp.swapaxes(stiffness, 0, 1), blocks)
    share = 2 * HB * pairs // peers
    stride = capacity + -(-share // chunks)

    def in_hbm(*arrays):
        return [pltpu.with_memory_space_constraint(x, pltpu.HBM) for x in arrays]

    send, slot = pl.pallas_call(
        functools.partial(prep_kernel, doms, peers, capacity, stride),
        out_shape=(shape((peers * (1 + share), LANES)), pltpu.HBM((cands, blocks), i32)),
        in_specs=[HBM] * 3,
        out_specs=(VMEM, HBM),
        scratch_shapes=[
            pltpu.VMEM((cands, blocks), i32),
            pltpu.VMEM((cands, blocks), i32),
            pltpu.VMEM(vec.shape[1:], F32),
            pltpu.VMEM(vec.shape[1:], F32),
            pltpu.VMEM((2 * HB * pairs, LANES), F32),
            pltpu.VMEM((cands, blocks), i32),
            pltpu.SemaphoreType.DMA((5,)),
        ],
        compiler_params=params(8),
        name="prep",
    )(*in_hbm(owners.T, local_seg.T, vec))

    def exchange(x, axis, size):
        x = x.reshape(size, peers // size * (1 + share), 1, LANES)
        x = lax.all_to_all(x, axis, split_axis=0, concat_axis=0, tiled=True)
        return x.reshape(peers * (1 + share), LANES)

    halfway = exchange(send, AXES[1], tools)
    halfway = pl.pallas_call(
        functools.partial(turn_kernel, doms, tools),
        out_shape=shape(halfway.shape),
        in_specs=[VMEM],
        out_specs=VMEM,
        compiler_params=params(4),
        name="turn",
    )(halfway)
    wanted = exchange(halfway, AXES[0], doms)

    parts = pl.pallas_call(
        parts_kernel,
        out_shape=shape((segs, PARTS * width), BF16),
        in_specs=[HBM] * 2,
        out_specs=VMEM,
        scratch_shapes=[pltpu.VMEM(tool_data.shape, F32), pltpu.SemaphoreType.DMA((1,))],
        compiler_params=params(8),
        cost_estimate=pl.CostEstimate(flops=1 << 20, bytes_accessed=4 << 20, transcendentals=0),
        name="parts",
    )(*in_hbm(slot, tool_data))

    rows_out = pl.pallas_call(
        functools.partial(rows_kernel, peers, capacity, stride),
        out_shape=shape((peers * stride * chunks, LANES)),
        in_specs=[VMEM] * 2,
        out_specs=VMEM,
        compiler_params=params(8),
        name="rows",
    )(wanted, parts)
    fetched = lax.all_to_all(
        rows_out.reshape(peers, stride, chunks, LANES), AXES, split_axis=0, concat_axis=0, tiled=True
    )

    wide = (blocks, NODE, LANES)
    left = (2 * NODE, nnz // 2 * 2 * NODE)
    inner, own, fields, slips, edges, rests = pl.pallas_call(
        main_kernel,
        out_shape=(
            pltpu.HBM(vec.shape, F32),
            pltpu.HBM(wide, BF16),
            shape(wide, BF16),
            shape((blocks // 2, NODE, LANES), BF16),
            shape((2 * HB,) + left, BF16),
            shape((2 * HB, NODE, LANES), BF16),
        ),
        in_specs=[HBM] * 5,
        out_specs=(HBM,) * 2 + (VMEM,) * 4,
        scratch_shapes=[
            pltpu.SMEM((nnz, blocks), i32),
            pltpu.VMEM(vec.shape, F32),
            pltpu.VMEM(rec.shape, F32),
            pltpu.VMEM(active.shape, i32),
            pltpu.VMEM(stiff.shape, F32),
            pltpu.VMEM((blocks + 2 * HB, NODE, LANES), BF16),
            pltpu.VMEM((SUB,) + left, BF16),
            pltpu.VMEM((SUB, NODE, LANES), BF16),
            pltpu.VMEM(vec.shape, F32),
            pltpu.VMEM(wide, BF16),
            pltpu.SemaphoreType.DMA((groups + 4,)),
            pltpu.SemaphoreType.DMA((2,)),
        ],
        compiler_params=params(20),
        cost_estimate=pl.CostEstimate(
            flops=6 * blocks * nnz * NODE * NODE * NVEC, bytes_accessed=24 << 20, transcendentals=0
        ),
        name="main",
    )(*in_hbm(columns.T, vec, rec, active, stiff))

    out = pl.pallas_call(
        functools.partial(contact_kernel, doms, tools, capacity, stride),
        out_shape=shape(vec.shape),
        in_specs=[HBM] * 4 + [VMEM] * 5,
        out_specs=VMEM,
        scratch_shapes=[
            pltpu.SMEM((cands, blocks), i32),
            pltpu.SMEM((nnz, blocks), i32),
            pltpu.VMEM(wide, BF16),
            pltpu.VMEM(vec.shape, F32),
            pltpu.VMEM((SUB, 2 * NODE, LANES), BF16),
            pltpu.VMEM((SUB, NODE, LANES), BF16),
            pltpu.VMEM((2 * HB * pairs, LANES), F32),
            pltpu.VMEM((2 * HB + 1, NODE, LANES), BF16),
            pltpu.VMEM((2 * HB, NODE, LANES), F32),
            pltpu.VMEM((2 * HB, pairs, LANES), F32),
            pltpu.SemaphoreType.DMA((2,)),
            pltpu.SemaphoreType.DMA((groups,)),
            pltpu.SemaphoreType.DMA((groups,)),
        ],
        compiler_params=params(16),
        cost_estimate=pl.CostEstimate(
            flops=80 * blocks * cands * NODE * NODE, bytes_accessed=4 << 20, transcendentals=2 * blocks * cands * NODE * NODE
        ),
        name="contact",
    )(*in_hbm(slot, columns.T, own, inner), fetched.reshape(peers * stride, chunks, LANES), fields, slips, edges, rests)
    out = out.reshape(groups, pairs, SUB, LANES)
    return jnp.swapaxes(out, 1, 2).reshape(blocks, NODE * NVEC)


def solution(mesh):
    split_rows = P(AXES, None)
    return jax.shard_map(
        per_device,
        mesh=mesh,
        in_specs=(split_rows,) * 5 + (P(AXES, None, None),) + (split_rows,) * 2,
        out_specs=split_rows,
        check_vma=False,
    )
```

profile of v0, /device:TPU:1, one launch (start us, length us, event | category | flops | bytes accessed | tf_op | source)
XLA Modules:
  0.0 48.2 jit_solution(4488588211481142026)
XLA Ops:
  0.0 1.5 %prep.1 = (f32[160,128]{1,0:T(8,128)S(1)}, s32[2,64]{1,0:T(2,128)}) custom-call(s32[2,64]{1,0:T(2,128)} %bitcast.43, s32[2,64]{1,0:T(2,128)} %bitcast.44, f32[8,256,128]{2,1,0:T(8,128)} %bitcast.38), custom_call_target="tpu_custom_call" | custom-call | tf_op jit(solution)/shard_map/prep/pallas_call | solution.py:521
  1.5 9.9 %all_to_all.15 = f32[4,40,1,128]{3,1,2,0:T(8,128)S(1)} all-to-all(f32[4,40,1,128]{3,1,2,0:T(8,128)S(1)} %bitcast.36), channel_id=1, replica_groups=mesh['dom'=8,'tool'=4] {'tool'}, dimensions={0} | all-to-all | bytes 163840 | tf_op jit(solution)/shard_map/all_to_all | solution.py:541
  11.3 0.6 %turn.1 = f32[160,128]{1,0:T(8,128)} custom-call(f32[160,128]{1,0:T(8,128)S(1)} %bitcast.34), custom_call_target="tpu_custom_call" | custom-call | tf_op jit(solution)/shard_map/turn/pallas_call | solution.py:545
  12.0 5.8 %all-to-all-start.1 = ((f32[8,20,1,128]{3,2,1,0:T(1,128)}), f32[8,20,1,128]{3,2,1,0:T(1,128)S(1)}, u32[]{:S(2)}, u32[]{:S(2)}) async-start(f32[8,20,1,128]{3,2,1,0:T(1,128)} %bitcast.18), calls=%async_computation.1 | async-start | bytes 163840 | tf_op jit(solution)/shard_map/all_to_all | solution.py:541
  17.8 1.2 %parts.1.part_ref = bf16[256,1536]{1,0:T(8,128)(2,1)S(1)} custom-call(s32[2,64]{1,0:T(2,128)} %get-tuple-element.13.after_prep.slot_hbm, f32[256,512]{1,0:T(8,128)} %tool_hbm.1), custom_call_target="tpu_custom_call" | custom-call | flops 1048576 | bytes 4194304 | tf_op jit(solution)/shard_map/parts/pallas_call | solution.py:555
  19.0 3.0 %all-to-all-done.1 = f32[8,20,1,128]{3,2,1,0:T(1,128)S(1)} async-done(((f32[8,20,1,128]{3,2,1,0:T(1,128)}), f32[8,20,1,128]{3,2,1,0:T(1,128)S(1)}, u32[]{:S(2)}, u32[]{:S(2)}) %all-to-all-start.1) | async-done | bytes 81952 | tf_op jit(solution)/shard_map/all_to_all | solution.py:541
  22.0 1.3 %rows.1 = f32[896,128]{1,0:T(8,128)} custom-call(f32[160,128]{1,0:T(8,128)S(1)} %bitcast.35, bf16[256,1536]{1,0:T(8,128)(2,1)S(1)} %parts.1.part_ref), custom_call_target="tpu_custom_call" | custom-call | tf_op jit(solution)/shard_map/rows/pallas_call | solution.py:566
  23.3 3.1 %all-to-all-start.2 = ((f32[32,7,4,128]{3,2,1,0:T(4,128)}), f32[32,7,4,128]{3,2,1,0:T(4,128)S(1)}, u32[]{:S(2)}, u32[]{:S(2)}) async-start(f32[32,7,4,128]{3,2,1,0:T(4,128)} %bitcast.20), calls=%async_computation.2 | async-start | bytes 917504 | tf_op jit(solution)/shard_map/all_to_all | solution.py:574
  26.4 12.1 %main.1 = (f32[8,256,128]{2,1,0:T(8,128)}, bf16[64,64,128]{2,1,0:T(8,128)(2,1)}, bf16[64,64,128]{2,1,0:T(8,128)(2,1)S(1)}, bf16[32,64,128]{2,1,0:T(8,128)(2,1)S(...) custom-call(s32[5,64]{1,0:T(8,128)} %bitcast.41, f32[8,256,128]{2,1,0:T(8,128)} %bitcast.39, ...), custom_call_target="tpu_custom_call" | custom-call | flops 503316480 | bytes 25165824 | tf_op jit(solution)/shard_map/main/pallas_call | solution.py:580
  38.5 2.0 %all-to-all-done.2 = f32[32,7,4,128]{3,2,1,0:T(4,128)S(1)} async-done(((f32[32,7,4,128]{3,2,1,0:T(4,128)}), f32[32,7,4,128]{3,2,1,0:T(4,128)S(1)}, u32[]{:S(2)}, u32[]{:S(2)}) %all-to-all-start.2) | async-done | bytes 458784 | tf_op jit(solution)/shard_map/all_to_all | solution.py:574
  40.5 7.7 %contact.1 = f32[8,256,128]{2,1,0:T(8,128)} custom-call(s32[2,64]{1,0:T(2,128)} %get-tuple-element.13.after_prep.slot_hbm, s32[5,64]{1,0:T(8,128)} %bitcast.42, bf16[64,64,128]{2,1,0:T(8,128)(2,1)} %get-tuple-element.14.own_hbm, f32[8,256,128]{2,1,0:T(8,128)} %get-tuple-element.15.inner_hbm, f32[224,4,128]{2,1,0:T(4,128)S(1)} %bitcast.33, ...), custom_call_target="tpu_custom_call" | custom-call | flops 41943040 | bytes 4194304 | tf_op jit(solution)/shard_map/contact/pallas_call | solution.py:613
Async XLA Ops:
  12.0 10.0 %all-to-all-start.1 = ((f32[8,20,1,128]{3,2,1,0:T(1,128)}), f32[8,20,1,128]{3,2,1,0:T(1,128)S(1)}, u32[]{:S(2)}, u32[]{:S(2)}) async-start(f32[8,20,1,128]{3,2,1,0:T(1,128)} %bitcast.18), calls=%async_computation.1 | async-start | bytes 163840 | tf_op jit(solution)/shard_map/all_to_all | solution.py:541
  23.3 17.2 %all-to-all-start.2 = ((f32[32,7,4,128]{3,2,1,0:T(4,128)}), f32[32,7,4,128]{3,2,1,0:T(4,128)S(1)}, u32[]{:S(2)}, u32[]{:S(2)}) async-start(f32[32,7,4,128]{3,2,1,0:T(4,128)} %bitcast.20), calls=%async_computation.2 | async-start | bytes 917504 | tf_op jit(solution)/shard_map/all_to_all | solution.py:574
where the time goes:
time: 48.6 us; the launch traced here: 48.2 us
  Pallas kernels  24.4 us (50%)
  blocking collectives  9.86 us (20%)
  starting transfers between devices  8.93 us (18%)
  waiting for transfers between devices  5 us (10%)
    pallas_call x1, Pallas kernels, per_device(): pl.pallas_call(main_kernel, out_shape=(pltpu.HBM(vec.shape, F32), pltpu.H...  12.1 us
    all_to_all x1, blocking collectives, exchange(): x = lax.all_to_all(x, axis, split_axis=0, concat_axis=0, tiled=True)  9.86 us
    pallas_call x1, Pallas kernels, per_device(): pl.pallas_call(functools.partial(contact_kernel, doms, tools, capacity, s...  7.73 us
    all_to_all x1, starting transfers between devices, exchange(): x = lax.all_to_all(x, axis, split_axis=0, concat_axis=0, tiled=True)  5.82 us
    all_to_all x1, starting transfers between devices, per_device(): lax.all_to_all(rows_out.reshape(peers, stride, chunks, LANES), AXES, spli...  3.11 us
    all_to_all x1, waiting for transfers between devices, exchange(): x = lax.all_to_all(x, axis, split_axis=0, concat_axis=0, tiled=True)  3 us
    all_to_all x1, waiting for transfers between devices, per_device(): lax.all_to_all(rows_out.reshape(peers, stride, chunks, LANES), AXES, spli...  2 us
    pallas_call x1, Pallas kernels, per_device(): pl.pallas_call(functools.partial(prep_kernel, doms, peers, capacity, stri...  1.47 us
  transfers between devices with their start and end apart: 2, of which 2 were waited for; matrix products, arithmetic and copies ran while one was open for 0% of the time, Pallas kernels for 27%

commit v1 on v0

--- a/solution.py
+++ b/solution.py
@@ -149,7 +149,8 @@
         places = jnp.where(hits, before + ranks(hits) - 1.0, -1.0)
         before = before + jnp.sum(hits.astype(F32), axis=1, keepdims=True)
         rank = jnp.sum(jnp.maximum(places, 0.0), axis=0, keepdims=True)
-        slot_ref[k : k + 1, :] = target * stride + rank.astype(jnp.int32)
+        tools = peers // doms
+        slot_ref[k : k + 1, :] = (target % tools * doms + target // tools) * stride + rank.astype(jnp.int32)
         wanted = jnp.broadcast_to(seg_ref[k : k + 1, :].astype(F32), (peers, blocks))
         for s in range(capacity):
             named = jnp.sum(jnp.where(places == float(s), wanted, 0.0), axis=1, keepdims=True)
@@ -167,15 +168,7 @@
     slots.wait()
 
 
-def turn_kernel(doms, tools, in_ref, out_ref):
-    rows = in_ref.shape[0] // (doms * tools)
-    for t in range(tools):
-        for d in range(doms):
-            source, target = (t * doms + d) * rows, (d * tools + t) * rows
-            out_ref[target : target + rows, :] = in_ref[source : source + rows, :]
-
-
-def rows_kernel(peers, capacity, stride, got_ref, part_ref, out_ref):
+def rows_kernel(doms, peers, capacity, stride, got_ref, part_ref, out_ref):
     segs, width = part_ref.shape[0], part_ref.shape[1] // PARTS
     chunks = width // LANES
     share = got_ref.shape[0] // peers - 1
@@ -194,8 +187,12 @@
     peer = lax.broadcasted_iota(jnp.int32, (peers, LANES), 0)
     for r in range(share):
         edge = got_ref[pl.ds(1 + r, peers, stride=1 + share), :]
-        following = jnp.where(peer == peers - 1, 0.0, pltpu.roll(edge, peers - 1, 0))
-        previous = jnp.where(peer == 0, 0.0, pltpu.roll(edge, 1, 0))
+        following = jnp.where(
+            peer < peers - doms, pltpu.roll(edge, peers - doms, 0), pltpu.roll(edge, peers - doms - 1, 0)
+        )
+        following = jnp.where(peer == peers - 1, 0.0, following)
+        previous = jnp.where(peer >= doms, pltpu.roll(edge, doms, 0), pltpu.roll(edge, doms + 1, 0))
+        previous = jnp.where(peer == 0, 0.0, previous)
         out_ref[pl.ds(capacity * chunks + r, peers, stride=stride * chunks), :] = jnp.where(
             me < peers // 2, following, previous
         )
@@ -359,14 +356,13 @@
 
 
 def contact_kernel(
-    doms, tools, capacity, stride,
+    peers, capacity, stride,
     slot_hbm, columns_hbm, own_hbm, inner_hbm, rows_ref, field_ref, slip_ref, edge_ref, rest_ref, out_ref,
     slot_ref, columns_ref, own_ref, inner_ref, tall_ref, gram_ref, halo_ref, wide_ref, hold_ref, delta_ref, sems, own_sems, inner_sems,
 ):
     got = copies_of((columns_hbm, slot_hbm), (columns_ref, slot_ref), sems)
     nnz, blocks = columns_ref.shape
     groups = blocks // SUB
-    peers = doms * tools
 
     def own_copy(g):
         spot = pl.ds(g * SUB, SUB)
@@ -443,8 +439,7 @@
         step = min(share, rows_ref.shape[1])
         for at in range(0, 2 * HB * pairs, step):
             q, r = at // share, at % share
-            p = q % doms * tools + q // doms
-            halo_ref[at : at + step, :] = rows_ref[p * stride + capacity + r // step][:step]
+            halo_ref[at : at + step, :] = rows_ref[q * stride + capacity + r // step][:step]
         for h in range(2 * HB):
             even, odd = doubled(halo_ref[h * pairs : (h + 1) * pairs, :], half)
             hold_ref[h, pl.ds(0, pairs, stride=2), :] = even
@@ -536,21 +531,9 @@
         name="prep",
     )(*in_hbm(owners.T, local_seg.T, vec))
 
-    def exchange(x, axis, size):
-        x = x.reshape(size, peers // size * (1 + share), 1, LANES)
-        x = lax.all_to_all(x, axis, split_axis=0, concat_axis=0, tiled=True)
-        return x.reshape(peers * (1 + share), LANES)
-
-    halfway = exchange(send, AXES[1], tools)
-    halfway = pl.pallas_call(
-        functools.partial(turn_kernel, doms, tools),
-        out_shape=shape(halfway.shape),
-        in_specs=[VMEM],
-        out_specs=VMEM,
-        compiler_params=params(4),
-        name="turn",
-    )(halfway)
-    wanted = exchange(halfway, AXES[0], doms)
+    members = AXES[::-1]
+    wanted = lax.all_to_all(send.reshape(peers, 1 + share, 1, LANES), members, split_axis=0, concat_axis=0, tiled=True)
+    wanted = wanted.reshape(peers * (1 + share), LANES)
 
     parts = pl.pallas_call(
         parts_kernel,
@@ -564,7 +547,7 @@
     )(*in_hbm(slot, tool_data))
 
     rows_out = pl.pallas_call(
-        functools.partial(rows_kernel, peers, capacity, stride),
+        functools.partial(rows_kernel, doms, peers, capacity, stride),
         out_shape=shape((peers * stride * chunks, LANES)),
         in_specs=[VMEM] * 2,
         out_specs=VMEM,
@@ -572,7 +555,7 @@
         name="rows",
     )(wanted, parts)
     fetched = lax.all_to_all(
-        rows_out.reshape(peers, stride, chunks, LANES), AXES, split_axis=0, concat_axis=0, tiled=True
+        rows_out.reshape(peers, stride, chunks, LANES), members, split_axis=0, concat_axis=0, tiled=True
     )
 
     wide = (blocks, NODE, LANES)
@@ -611,7 +594,7 @@
     )(*in_hbm(columns.T, vec, rec, active, stiff))
 
     out = pl.pallas_call(
-        functools.partial(contact_kernel, doms, tools, capacity, stride),
+        functools.partial(contact_kernel, peers, capacity, stride),
         out_shape=shape(vec.shape),
         in_specs=[HBM] * 4 + [VMEM] * 5,
         out_specs=VMEM,

time: 48.6 us -> 43.3 us (0.89)
  the two profiles are of different devices: /device:TPU:1 before, /device:TPU:0 now
where the time goes in v1:
time: 43.3 us; the launch traced here: 43 us
  Pallas kernels  24.4 us (56%)
  starting transfers between devices  9.9 us (23%)
  waiting for transfers between devices  8.7 us (20%)
    pallas_call x1, Pallas kernels, per_device(): pl.pallas_call(main_kernel, out_shape=(pltpu.HBM(vec.shape, F32), pltpu.H...  12.1 us
    pallas_call x1, Pallas kernels, per_device(): pl.pallas_call(functools.partial(contact_kernel, peers, capacity, stride)...  7.72 us
    all_to_all x1, starting transfers between devices, per_device(): lax.all_to_all(send.reshape(peers, 1 + share, 1, LANES), members, split_a...  7.3 us
    all_to_all x1, waiting for transfers between devices, per_device(): lax.all_to_all(send.reshape(peers, 1 + share, 1, LANES), members, split_a...  6.39 us
    all_to_all x1, starting transfers between devices, per_device(): lax.all_to_all(rows_out.reshape(peers, stride, chunks, LANES), members, s...  2.6 us
    all_to_all x1, waiting for transfers between devices, per_device(): lax.all_to_all(rows_out.reshape(peers, stride, chunks, LANES), members, s...  2.3 us
    pallas_call x1, Pallas kernels, per_device(): pl.pallas_call(functools.partial(prep_kernel, doms, peers, capacity, stri...  2.11 us
    pallas_call x1, Pallas kernels, per_device(): pl.pallas_call(functools.partial(rows_kernel, doms, peers, capacity, stri...  1.29 us
  transfers between devices with their start and end apart: 2, of which 2 were waited for; matrix products, arithmetic and copies ran while one was open for 0% of the time, Pallas kernels for 31%

profile of v1, /device:TPU:0, one launch (start us, length us, event | category | flops | bytes accessed | tf_op | source)
XLA Modules:
  0.0 43.0 jit_solution(16620636257697592262)
XLA Ops:
  0.0 2.1 %prep.1 = (f32[160,128]{1,0:T(8,128)}, s32[2,64]{1,0:T(2,128)}) custom-call(s32[2,64]{1,0:T(2,128)} %bitcast.37, s32[2,64]{1,0:T(2,128)} %bitcast.38, f32[8,256,128]{2,1,0:T(8,128)} %bitcast.32), custom_call_target="tpu_custom_call" | custom-call | tf_op jit(solution)/shard_map/prep/pallas_call | solution.py:516
  2.1 7.3 %all-to-all-start = ((f32[32,5,1,128]{3,2,1,0:T(1,128)}), f32[32,5,1,128]{3,2,1,0:T(1,128)S(1)}, u32[]{:S(2)}, u32[]{:S(2)}) async-start(f32[32,5,1,128]{3,2,1,0:T(1,128)} %bitcast.15), calls=%async_computation | async-start | bytes 163840 | tf_op jit(solution)/shard_map/all_to_all | solution.py:535
  9.4 1.2 %parts.1.part_ref = bf16[256,1536]{1,0:T(8,128)(2,1)S(1)} custom-call(s32[2,64]{1,0:T(2,128)} %get-tuple-element.13.after_prep.slot_hbm, f32[256,512]{1,0:T(8,128)} %tool_hbm.1), custom_call_target="tpu_custom_call" | custom-call | flops 1048576 | bytes 4194304 | tf_op jit(solution)/shard_map/parts/pallas_call | solution.py:538
  10.6 6.4 %all-to-all-done = f32[32,5,1,128]{3,2,1,0:T(1,128)S(1)} async-done(((f32[32,5,1,128]{3,2,1,0:T(1,128)}), f32[32,5,1,128]{3,2,1,0:T(1,128)S(1)}, u32[]{:S(2)}, u32[]{:S(2)}) %all-to-all-start) | async-done | bytes 81952 | tf_op jit(solution)/shard_map/all_to_all | solution.py:535
  17.0 1.3 %rows.1 = f32[896,128]{1,0:T(8,128)} custom-call(f32[160,128]{1,0:T(8,128)S(1)} %bitcast.30, bf16[256,1536]{1,0:T(8,128)(2,1)S(1)} %parts.1.part_ref), custom_call_target="tpu_custom_call" | custom-call | tf_op jit(solution)/shard_map/rows/pallas_call | solution.py:549
  18.3 2.6 %all-to-all-start.1 = ((f32[32,7,4,128]{3,2,1,0:T(4,128)}), f32[32,7,4,128]{3,2,1,0:T(4,128)S(1)}, u32[]{:S(2)}, u32[]{:S(2)}) async-start(f32[32,7,4,128]{3,2,1,0:T(4,128)} %bitcast.17), calls=%async_computation.1 | async-start | bytes 917504 | tf_op jit(solution)/shard_map/all_to_all | solution.py:557
  20.9 12.1 %main.1 = (f32[8,256,128]{2,1,0:T(8,128)}, bf16[64,64,128]{2,1,0:T(8,128)(2,1)}, bf16[64,64,128]{2,1,0:T(8,128)(2,1)S(1)}, bf16[32,64,128]{2,1,0:T(8,128)(2,1)S(...) custom-call(s32[5,64]{1,0:T(8,128)} %bitcast.35, f32[8,256,128]{2,1,0:T(8,128)} %bitcast.33, ...), custom_call_target="tpu_custom_call" | custom-call | flops 503316480 | bytes 25165824 | tf_op jit(solution)/shard_map/main/pallas_call | solution.py:563
  33.0 2.3 %all-to-all-done.1 = f32[32,7,4,128]{3,2,1,0:T(4,128)S(1)} async-done(((f32[32,7,4,128]{3,2,1,0:T(4,128)}), f32[32,7,4,128]{3,2,1,0:T(4,128)S(1)}, u32[]{:S(2)}, u32[]{:S(2)}) %all-to-all-start.1) | async-done | bytes 458784 | tf_op jit(solution)/shard_map/all_to_all | solution.py:557
  35.3 7.7 %contact.1 = f32[8,256,128]{2,1,0:T(8,128)} custom-call(s32[2,64]{1,0:T(2,128)} %get-tuple-element.13.after_prep.slot_hbm, s32[5,64]{1,0:T(8,128)} %bitcast.36, bf16[64,64,128]{2,1,0:T(8,128)(2,1)} %get-tuple-element.14.own_hbm, f32[8,256,128]{2,1,0:T(8,128)} %get-tuple-element.15.inner_hbm, f32[224,4,128]{2,1,0:T(4,128)S(1)} %bitcast.29, ...), custom_call_target="tpu_custom_call" | custom-call | flops 41943040 | bytes 4194304 | tf_op jit(solution)/shard_map/contact/pallas_call | solution.py:596
Async XLA Ops:
  2.1 14.9 %all-to-all-start = ((f32[32,5,1,128]{3,2,1,0:T(1,128)}), f32[32,5,1,128]{3,2,1,0:T(1,128)S(1)}, u32[]{:S(2)}, u32[]{:S(2)}) async-start(f32[32,5,1,128]{3,2,1,0:T(1,128)} %bitcast.15), calls=%async_computation | async-start | bytes 163840 | tf_op jit(solution)/shard_map/all_to_all | solution.py:535
  18.3 17.0 %all-to-all-start.1 = ((f32[32,7,4,128]{3,2,1,0:T(4,128)}), f32[32,7,4,128]{3,2,1,0:T(4,128)S(1)}, u32[]{:S(2)}, u32[]{:S(2)}) async-start(f32[32,7,4,128]{3,2,1,0:T(4,128)} %bitcast.17), calls=%async_computation.1 | async-start | bytes 917504 | tf_op jit(solution)/shard_map/all_to_all | solution.py:557
